TPU v7x, 32 devices: a whole 2x2x4 slice. The times are simulated.
32 devices in a mesh: groups: 2 (over y), tp: 4 (over z), rep: 4 (over x, core).
Axes of the slice: x: 2, y: 2, z: 4, core: 2. Of those that a mesh axis runs over, the one named last changes fastest.
Arguments:
- tokens: bfloat16 [2, 32, 16384], P(None, ('groups', 'tp'), 'rep'), parts along dimension 1, may hold values from -6 to 6
- query_weight: bfloat16 [16384, 16384], P('rep', 'tp'), may hold values from -0.046875 to 0.046875
- key_value_weight: bfloat16 [16384, 2048], P('rep', 'tp'), may hold values from -0.046875 to 0.046875
- adapter_down_weight: bfloat16 [8, 16384, 16], P(('groups', 'tp'), 'rep'), parts along dimension 0, may hold values from -0.046875 to 0.046875
- adapter_up_weight: bfloat16 [8, 16, 16384], P(('groups', 'rep'), None, 'tp'), parts along dimension 0, may hold values from -1.5 to 1.5
- request_tenant: int32 [32, 1], P('groups'), parts along dimension 0, may hold values from 0 to 3; in each aligned block of 16 rows (0 to 15, 16 to 31, ...) at most 12 rows name the same one
- tenant_adapter_slot: int32 [4], replicated, may hold values from 0 to 3, each once
- key_value_cache: bfloat16 [32, 192, 2048], P(('groups', 'tp', 'rep')), parts along dimension 0, may hold values from -110 to 110
- cache_length_per_row: int32 [32], P(('groups', 'tp', 'rep')), parts along dimension 0, may hold values from 1 to 192, 1536 in all
Outputs:
- attended: bfloat16 [2, 32, 16384], P(None, ('groups', 'tp', 'rep')), parts along dimension 1
There are 2 independent parts, one for each index of `groups`. A program takes and returns all parts, laid end to end along the dimension named above; an argument that names none is the same for every part. Nothing has to cross between parts.
Inputs may be any that keep to these rules, and one draw needn't show every extreme that they name: `request_tenant`: every tenant has a request; the busiest tenant has exactly 12 requests. `tenant_adapter_slot`: each slot holds the adapters of exactly one tenant. `cache_length_per_row`: some request has exactly 192 cached positions.
All inputs are finite; a program needn't handle non-finite values. No bound on the sum of `cache_length_per_row` on one device may be relied on, other than what follows from the above.
Results may differ from a plain program's by a relative error of at most 0.012.
The roundings to bfloat16 on the way count: a program that leaves them out, or rounds other values in their place, can miss the bound.
Values may be sent and summed in bfloat16 or wider, within the bound.
A program may use at most 128 MiB of HBM per device.

v0:
```python
import jax
import jax.numpy as jnp
from jax import lax
from jax.sharding import PartitionSpec as P

KEY_VALUE_HEADS = 8
HEAD_SIZE = 128


def slot_lookup(request_tenant, tenant_adapter_slot):
    labels = jnp.arange(tenant_adapter_slot.shape[0], dtype=jnp.int32)
    return jnp.sum(
        jnp.where(request_tenant == labels[None, :], tenant_adapter_slot[None, :], 0), axis=1
    )


def attend(query_matrix, incoming_key_value, key_value_cache, cache_length_per_row):
    row_indices = query_matrix.shape[0]
    position_span = key_value_cache.shape[1]
    incoming_token = incoming_key_value.shape[0]
    half_width = KEY_VALUE_HEADS * HEAD_SIZE
    head_outputs = query_matrix.reshape(row_indices, KEY_VALUE_HEADS, -1, HEAD_SIZE)
    stored_keys = key_value_cache[:, :, :half_width].reshape(
        row_indices, position_span, KEY_VALUE_HEADS, HEAD_SIZE
    )
    stored_values = key_value_cache[:, :, half_width:].reshape(
        row_indices, position_span, KEY_VALUE_HEADS, HEAD_SIZE
    )
    incoming_keys = jnp.transpose(incoming_key_value[:, :, :half_width], (1, 0, 2)).reshape(
        row_indices, incoming_token, KEY_VALUE_HEADS, HEAD_SIZE
    )
    incoming_values = jnp.transpose(incoming_key_value[:, :, half_width:], (1, 0, 2)).reshape(
        row_indices, incoming_token, KEY_VALUE_HEADS, HEAD_SIZE
    )
    scale = HEAD_SIZE ** (-0.5)
    older = (
        jnp.einsum("bgmd,bjgd->bgmj", head_outputs, stored_keys, preferred_element_type=jnp.float32)
        * scale
    )
    newer = (
        jnp.einsum(
            "bgmd,bjgd->bgmj", head_outputs, incoming_keys, preferred_element_type=jnp.float32
        )
        * scale
    )
    valid = jnp.arange(position_span, dtype=jnp.int32)[None, :] < cache_length_per_row[:, None]
    older = jnp.where(valid[:, None, None, :], older, -jnp.inf)
    top = jnp.maximum(jnp.max(older, axis=-1), jnp.max(newer, axis=-1))[..., None]
    older_exp = jnp.exp(older - top)
    newer_exp = jnp.exp(newer - top)
    total = jnp.sum(older_exp, axis=-1, keepdims=True) + jnp.sum(newer_exp, axis=-1, keepdims=True)
    older_prob = (older_exp / total).astype(jnp.bfloat16)
    newer_prob = (newer_exp / total).astype(jnp.bfloat16)
    mixed = jnp.einsum(
        "bgmj,bjgd->bgmd", older_prob, stored_values, preferred_element_type=jnp.float32
    )
    mixed = mixed + jnp.einsum(
        "bgmj,bjgd->bgmd", newer_prob, incoming_values, preferred_element_type=jnp.float32
    )
    return mixed.astype(jnp.bfloat16).reshape(row_indices, -1)


def shards(
    tokens,
    query_weight,
    key_value_weight,
    adapter_down_weight,
    adapter_up_weight,
    request_tenant,
    tenant_adapter_slot,
    key_value_cache,
    cache_length_per_row,
):
    tp_count = lax.axis_size("tp")
    rep_count = lax.axis_size("rep")
    rep_place = lax.axis_index("rep")
    rows_all = request_tenant.shape[0]
    request_slots = adapter_down_weight.shape[0]
    replicated_slots = adapter_up_weight.shape[0]
    adapter_rank_size = adapter_down_weight.shape[2]
    query_columns = query_weight.shape[1]
    kv_cols = key_value_weight.shape[1]
    local_rows = rows_all // (tp_count * rep_count)
    slot_row = slot_lookup(request_tenant, tenant_adapter_slot)
    flattened_down_weight = jnp.transpose(adapter_down_weight, (1, 0, 2)).reshape(
        adapter_down_weight.shape[1], request_slots * adapter_rank_size
    )
    flattened_up_weight = adapter_up_weight.reshape(
        replicated_slots * adapter_rank_size, query_columns
    )
    rep_labels = rep_place * replicated_slots + jnp.arange(replicated_slots, dtype=jnp.int32)
    rep_match = slot_row[:, None] == rep_labels[None, :]
    steps = tokens.shape[0]
    count = tokens.shape[0]
    piece = lax.all_gather(tokens, "tp", axis=1, tiled=True)
    flat = piece.reshape(-1, piece.shape[2])
    joined = jnp.concatenate(
        [
            jnp.dot(flat, query_weight, preferred_element_type=jnp.float32),
            jnp.dot(flat, key_value_weight, preferred_element_type=jnp.float32),
            jnp.dot(flat, flattened_down_weight, preferred_element_type=jnp.float32),
        ],
        axis=1,
    )
    terms = joined.reshape(piece.shape[0], piece.shape[1], -1)
    q_part = terms[:, :, :query_columns]
    kv_part = terms[:, :, query_columns : query_columns + kv_cols]
    low_part = terms[:, :, query_columns + kv_cols :]
    low_sum = lax.psum(low_part, "rep")
    low_all = lax.all_gather(low_sum.astype(jnp.bfloat16), "tp", axis=2, tiled=True)
    low_rep = lax.dynamic_slice_in_dim(
        low_all,
        rep_place * replicated_slots * adapter_rank_size,
        replicated_slots * adapter_rank_size,
        2,
    )
    low_rep = low_rep.reshape(count, rows_all, replicated_slots, adapter_rank_size)
    masked = jnp.where(rep_match[None, :, :, None], low_rep, jnp.zeros((), jnp.bfloat16))
    delta = jnp.dot(
        masked.reshape(count * rows_all, replicated_slots * adapter_rank_size),
        flattened_up_weight,
        preferred_element_type=jnp.float32,
    )
    q_part = (q_part + delta.reshape(count, rows_all, query_columns)).reshape(
        count, tp_count, rep_count * local_rows, query_columns
    )
    kv_part = kv_part.reshape(count, tp_count, rep_count * local_rows, kv_cols)
    q_sum = lax.psum_scatter(q_part, "rep", scatter_dimension=2, tiled=True)
    kv_sum = lax.psum_scatter(kv_part, "rep", scatter_dimension=2, tiled=True)
    query_vector = lax.all_to_all(
        q_sum.astype(jnp.bfloat16), "tp", split_axis=1, concat_axis=3, tiled=True
    )
    key_value_rows = lax.all_to_all(
        kv_sum.astype(jnp.bfloat16), "tp", split_axis=1, concat_axis=3, tiled=True
    )
    query_vector, key_value_rows = (
        query_vector.reshape(count, local_rows, -1),
        key_value_rows.reshape(count, local_rows, -1),
    )
    results = []
    for step in range(steps):
        results.append(
            attend(
                query_vector[step],
                key_value_rows[: step + 1],
                key_value_cache,
                cache_length_per_row,
            )
        )
    return jnp.stack(results)


def solution(mesh):
    placed = (
        P(None, ("groups", "tp"), "rep"),
        P("rep", "tp"),
        P("rep", "tp"),
        P(("groups", "tp"), "rep", None),
        P(("groups", "rep"), None, "tp"),
        P("groups", None),
        P(),
        P(("groups", "tp", "rep"), None, None),
        P(("groups", "tp", "rep")),
    )
    return jax.shard_map(
        shards,
        mesh=mesh,
        in_specs=placed,
        out_specs=P(None, ("groups", "tp", "rep"), None),
        check_vma=False,
    )
```

profile of v0, /device:TPU:0, one launch (start us, length us, event | category | flops | bytes accessed | tf_op | source)
XLA Modules:
  0.0 101.1 jit_solution(14843845398292684022)
XLA Ops:
  0.0 0.0 copy-start
  0.0 0.0 copy-start.4
  0.0 0.0 copy-start.2
  0.0 0.0 copy-start.3
  0.0 0.0 copy-start.1
  0.0 1.0 copy.66
  1.0 15.6 %all_gather.6 = bf16[2,16,4096]{2,0,1:T(2,128)(2,1)S(1)} all-gather(bf16[2,4,4096]{2,0,1:T(2,128)(2,1)S(1)} %copy.66), channel_id=1, replica_groups=mesh['groups'=2,'tp'=4,'rep'=4] {'tp'}, dimensions={1}, use_global_device_ids=true | all-gather | bytes 327680 | tf_op jit(solution)/shard_map/all_gather | solution.py:95
  16.7 0.1 copy.67
  16.8 1.1 %fusion.10 = f32[32,16]{1,0:T(8,128)S(1)} fusion(bf16[32,4096]{1,0:T(8,128)(2,1)S(1)} %bitcast.53, bf16[1,4096,16]{1,2,0:T(8,128)(2,1)} %param.12), kind=kOutput, calls=%fused_computation.20 | convolution fusion | flops 4194304 | bytes 395264 | tf_op jit(solution)/shard_map/dot_general | solution.py:101
  17.9 3.0 %fusion.29 = f32[32,512]{1,0:T(8,128)S(1)} fusion(bf16[32,4096]{1,0:T(8,128)(2,1)S(1)} %bitcast.54, bf16[4096,512]{1,0:T(8,128)(2,1)} %param.11), kind=kOutput, calls=%fused_computation.61 | convolution fusion | flops 134217728 | bytes 4521984 | tf_op jit(solution)/shard_map/dot_general | solution.py:100
  20.9 13.5 %fusion.28 = f32[32,4096]{1,0:T(8,128)S(1)} fusion(bf16[32,4096]{1,0:T(8,128)(2,1)S(1)} %bitcast.55, bf16[4096,4096]{1,0:T(8,128)(2,1)} %param.10), kind=kOutput, calls=%fused_computation.60 | convolution fusion | flops 1073741824 | bytes 34340864 | tf_op jit(solution)/shard_map/dot_general | solution.py:99
  34.6 0.0 copy-done.2
  34.6 0.0 copy-done.3
  34.6 0.1 select_reduce_fusion
  34.7 10.1 %psum.7 = bf16[2,16,16]{2,1,0:T(8,128)(2,1)S(1)} all-reduce(f32[2,16,16]{2,1,0:T(8,128)S(1)} %slice.59), channel_id=1, replica_groups=mesh['groups'=2,'tp'=4,'rep'=4] {'rep'}, use_global_device_ids=true, to_apply=%region_1.2 | all-reduce | flops 512 | bytes 3072 | tf_op jit(solution)/shard_map/psum | solution.py:109
  44.8 0.1 copy.69
  44.9 13.2 %all_gather.7 = bf16[2,16,64]{1,0,2:T(2,128)(2,1)S(1)} all-gather(bf16[2,16,16]{1,0,2:T(2,128)(2,1)S(1)} %copy.69), channel_id=1, replica_groups=mesh['groups'=2,'tp'=4,'rep'=4] {'tp'}, dimensions={2}, use_global_device_ids=true | all-gather | bytes 5120 | tf_op jit(solution)/shard_map/all_gather | solution.py:110
  58.1 0.0 copy-done
  58.1 0.2 convolution_add_fusion
  58.4 0.1 reshape.221
  58.5 0.3 copy.71
  58.9 0.0 copy-done.4
  59.0 0.6 dynamic-slice
  59.5 17.1 %all-reduce.4 = (bf16[2,4,4,4096]{3,1,2,0:T(4,128)(2,1)S(1)}, bf16[2,4,4,512]{3,1,0,2:T(4,128)(2,1)S(1)}) all-reduce(f32[2,4,4,4096]{3,1,2,0:T(4,128)S(1)} %copy.71, f32[2,4,4,512]{3,1,0,2:T(4,128)S(1)} %copy.74), channel_id=2, replica_groups=mesh['groups'=2,'tp'=4,'rep'=4] {'rep'}, use_global_device_ids=true, to_apply=%region_2.3.clone | all-reduce | flops 147456 | bytes 884736
  76.6 0.7 dynamic-slice_convert_fusion.1
  77.3 0.6 copy.75
  77.9 5.1 %all-to-all-start.1 = ((bf16[2,4,1,512]{3,0,2,1:T(2,128)(2,1)}), bf16[2,4,1,512]{3,0,2,1:T(2,128)(2,1)S(1)}, u32[]{:S(2)}, u32[]{:S(2)}) async-start(bf16[2,4,1,512]{3,0,2,1:T(2,128)(2,1)} %copy.75), calls=%async_computation.1 | async-start | bytes 16384 | tf_op jit(solution)/shard_map/all_to_all | solution.py:133
  83.6 0.7 dynamic-slice_convert_fusion
  84.3 0.0 copy-done.1
  84.3 0.1 slice_bitcast_fusion.1
  84.4 0.7 copy.72
  85.1 0.1 copy.86
  85.2 0.1 copy.87
  85.2 3.3 %all-to-all-done.1 = bf16[2,4,1,512]{3,0,2,1:T(2,128)(2,1)S(1)} async-done(((bf16[2,4,1,512]{3,0,2,1:T(2,128)(2,1)}), bf16[2,4,1,512]{3,0,2,1:T(2,128)(2,1)S(1)}, u32[]{:S(2)}, u32[]{:S(2)}) %all-to-all-start.1) | async-done | bytes 8224 | tf_op jit(solution)/shard_map/all_to_all | solution.py:133
  88.6 3.3 %all-to-all-start = ((bf16[2,4,1,4096]{3,0,2,1:T(2,128)(2,1)}), bf16[2,4,1,4096]{3,0,2,1:T(2,128)(2,1)S(1)}, u32[]{:S(2)}, u32[]{:S(2)}) async-start(bf16[2,4,1,4096]{3,0,2,1:T(2,128)(2,1)} %copy.72), calls=%async_computation | async-start | bytes 131072 | tf_op jit(solution)/shard_map/all_to_all | solution.py:130
  91.9 5.7 %all-to-all-done = bf16[2,4,1,4096]{3,0,2,1:T(2,128)(2,1)S(1)} async-done(((bf16[2,4,1,4096]{3,0,2,1:T(2,128)(2,1)}), bf16[2,4,1,4096]{3,0,2,1:T(2,128)(2,1)S(1)}, u32[]{:S(2)}, u32[]{:S(2)}) %all-to-all-start) | async-done | bytes 65568 | tf_op jit(solution)/shard_map/all_to_all | solution.py:130
  97.6 0.3 slice_reduce_fusion.1
  97.9 0.1 fusion.20
  98.1 0.4 fusion.27
  98.5 0.4 fusion.25
  98.9 0.2 fusion.26
  99.0 0.2 fusion.12
  99.3 0.2 fusion.13
  99.5 0.3 fusion.4
  99.8 0.2 fusion.2
  100.0 0.3 fusion.3
  100.3 0.8 pad_maximum_fusion.1
  (18 shorter events, 0.3 us)
Async XLA Ops:
  0.0 58.1 %copy-start = (bf16[1,16,4096]{2,1,0:T(8,128)(2,1)S(1)}, bf16[1,16,4096]{2,1,0:T(8,128)(2,1)}, u32[]{:S(2)}) copy-start(bf16[1,16,4096]{2,1,0:T(8,128)(2,1)} %param.13) | copy-start | bytes 393220
  0.0 58.9 %copy-start.4 = (u32[32]{0:T(128)S(1)}, u32[32]{0:T(128)}, u32[]{:S(2)}) copy-start(u32[32]{0:T(128)} %constant.27) | copy-start | bytes 388
  0.0 34.5 %copy-start.2 = (s32[4]{0:T(128)S(1)}, s32[4]{0:T(128)}, u32[]{:S(2)}) copy-start(s32[4]{0:T(128)} %param.15) | copy-start | bytes 52
  0.0 34.6 %copy-start.3 = (s32[16,1]{0,1:T(1,128)S(1)}, s32[16,1]{0,1:T(1,128)}, u32[]{:S(2)}) copy-start(s32[16,1]{0,1:T(1,128)} %param.14) | copy-start | bytes 196
  0.0 84.3 %copy-start.1 = (bf16[1,192,2048]{2,1,0:T(8,128)(2,1)S(1)}, bf16[1,192,2048]{2,1,0:T(8,128)(2,1)}, u32[]{:S(2)}) copy-start(bf16[1,192,2048]{2,1,0:T(8,128)(2,1)} %param.16) | copy-start | bytes 2359300
  77.9 10.7 %all-to-all-start.1 = ((bf16[2,4,1,512]{3,0,2,1:T(2,128)(2,1)}), bf16[2,4,1,512]{3,0,2,1:T(2,128)(2,1)S(1)}, u32[]{:S(2)}, u32[]{:S(2)}) async-start(bf16[2,4,1,512]{3,0,2,1:T(2,128)(2,1)} %copy.75), calls=%async_computation.1 | async-start | bytes 16384 | tf_op jit(solution)/shard_map/all_to_all | solution.py:133
  88.6 9.0 %all-to-all-start = ((bf16[2,4,1,4096]{3,0,2,1:T(2,128)(2,1)}), bf16[2,4,1,4096]{3,0,2,1:T(2,128)(2,1)S(1)}, u32[]{:S(2)}, u32[]{:S(2)}) async-start(bf16[2,4,1,4096]{3,0,2,1:T(2,128)(2,1)} %copy.72), calls=%async_computation | async-start | bytes 131072 | tf_op jit(solution)/shard_map/all_to_all | solution.py:130
where the time goes:
time: 101 us
  blocking collectives  56 us (55%)
  matrix products  19.7 us (20%)
  waiting for transfers between devices  9.03 us (9%)
  starting transfers between devices  8.37 us (8%)
  local copies, waits for them, and re-layouts  5.61 us (6%)
  other arithmetic  1.35 us (1%)
    unnamed x1, blocking collectives  17.1 us
    all_gather x1, blocking collectives, shards(): piece = lax.all_gather(tokens, 'tp', axis=1, tiled=True)  15.6 us
    dot_general x1, matrix products, shards(): jnp.dot(flat, query_weight, preferred_element_type=jnp.float32)  13.5 us
    all_gather x1, blocking collectives, shards(): lax.all_gather(low_sum.astype(jnp.bfloat16), 'tp', axis=2, tiled=True)  13.2 us
    psum x1, blocking collectives, shards(): low_sum = lax.psum(low_part, 'rep')  10.1 us
    all_to_all x1, waiting for transfers between devices, shards(): lax.all_to_all(q_sum.astype(jnp.bfloat16), 'tp', split_axis=1, concat_axi...  5.7 us
    all_to_all x1, starting transfers between devices, shards(): lax.all_to_all(kv_sum.astype(jnp.bfloat16), 'tp', split_axis=1, concat_ax...  5.09 us
    all_to_all x1, waiting for transfers between devices, shards(): lax.all_to_all(kv_sum.astype(jnp.bfloat16), 'tp', split_axis=1, concat_ax...  3.33 us
  transfers between devices with their start and end apart: 2, of which 2 were waited for; matrix products, arithmetic and copies ran while one was open for 2% of the time, Pallas kernels for 0%

commit v1 on v0

--- a/solution.py
+++ b/solution.py
@@ -1,10 +1,459 @@
+import functools
+
 import jax
 import jax.numpy as jnp
 from jax import lax
+from jax.experimental import pallas as pl
+from jax.experimental.pallas import tpu as pltpu
 from jax.sharding import PartitionSpec as P
 
 KEY_VALUE_HEADS = 8
 HEAD_SIZE = 128
+CHUNK = 512
+DEFER = 2
+MESH = pl.DeviceIdType.MESH
+
+
+def peer(tp, rep):
+    return {"tp": tp, "rep": rep}
+
+
+def remote(src, dst, send_sem, recv_sem, tp, rep):
+    return pltpu.make_async_remote_copy(
+        src_ref=src,
+        dst_ref=dst,
+        send_sem=send_sem,
+        recv_sem=recv_sem,
+        device_id=peer(tp, rep),
+        device_id_type=MESH,
+    )
+
+
+def fused_kernel(
+    tp_count,
+    rep_count,
+    tokens,
+    query_weight,
+    key_value_weight,
+    adapter_down_weight,
+    adapter_up_weight,
+    request_tenant,
+    tenant_adapter_slot,
+    key_value_cache,
+    cache_length,
+    out,
+    own_tokens,
+    own_wide,
+    gathered,
+    hidden,
+    weights,
+    down,
+    up,
+    cache,
+    low_send,
+    low_recv,
+    low_masked,
+    held,
+    part_send,
+    part_recv,
+    stage,
+    query_send,
+    query_recv,
+    kv_send,
+    kv_recv,
+    weight_sem,
+    load_sem,
+    gather_send_sem,
+    gather_recv_sem,
+    low_send_sem,
+    low_recv_sem,
+    part_send_sem,
+    part_recv_sem,
+    query_send_sem,
+    query_recv_sem,
+    kv_send_sem,
+    kv_recv_sem,
+):
+    t = lax.axis_index("tp")
+    r = lax.axis_index("rep")
+    steps, rows_rep, depth = tokens.shape
+    half_depth = depth // 2
+    group_rows = steps * tp_count
+    rows = group_rows * rep_count
+    query_columns = query_weight.shape[1]
+    query_chunks = query_columns // CHUNK
+    chunk_heads = CHUNK // HEAD_SIZE
+    rank = adapter_down_weight.shape[2]
+    positions = key_value_cache.shape[1]
+    half_width = KEY_VALUE_HEADS * HEAD_SIZE
+
+    barrier = pltpu.get_barrier_semaphore()
+    for dt in range(tp_count):
+        for dr in range(rep_count):
+            if dt or dr:
+                pl.semaphore_signal(
+                    barrier,
+                    inc=1,
+                    device_id=peer(lax.rem(t + dt, tp_count), lax.rem(r + dr, rep_count)),
+                    device_id_type=MESH,
+                )
+
+    load_tokens = pltpu.make_async_copy(tokens, own_tokens, load_sem.at[0])
+    load_down = pltpu.make_async_copy(adapter_down_weight.at[0], down, load_sem.at[1])
+    load_up = pltpu.make_async_copy(adapter_up_weight.at[0], up, load_sem.at[2])
+    load_cache = pltpu.make_async_copy(key_value_cache.at[0], cache, load_sem.at[3])
+    load_tokens.start()
+    load_down.start()
+    load_weights = [
+        pltpu.make_async_copy(key_value_weight, weights.at[0], weight_sem.at[0])
+    ] + [
+        pltpu.make_async_copy(
+            query_weight.at[:, pl.ds(c * CHUNK, CHUNK)], weights.at[c + 1], weight_sem.at[c + 1]
+        )
+        for c in range(query_chunks)
+    ]
+    load_weights[0].start()
+    load_up.start()
+    for copy in load_weights[1:]:
+        copy.start()
+    load_cache.start()
+
+    load_tokens.wait()
+    for s in range(steps):
+        wide = own_tokens[s].astype(jnp.float32)
+        for h in range(2):
+            first = h * steps * rows_rep + s * rows_rep
+            own_wide[first : first + rows_rep, :] = wide[:, h * half_depth : (h + 1) * half_depth]
+    gathered[t] = own_wide[...].astype(jnp.bfloat16)
+    pl.semaphore_wait(barrier, tp_count * rep_count - 1)
+
+    sends = []
+    gathers = []
+    for d in range(tp_count - 1, 0, -1):
+        to = lax.rem(t + d, tp_count)
+        copy = remote(
+            gathered.at[t], gathered.at[t], gather_send_sem.at[to], gather_recv_sem.at[t], to, r
+        )
+        copy.start()
+        sends.append(copy)
+        gathers.append(
+            remote(
+                gathered.at[to], gathered.at[to], gather_send_sem.at[to], gather_recv_sem.at[to], to, r
+            )
+        )
+
+    row = lax.broadcasted_iota(jnp.int32, (rows, HEAD_SIZE), 0)
+    request = lax.rem(row // steps, tp_count) * rep_count + row // group_rows
+    tenant = jnp.zeros_like(row)
+    for i in range(tp_count * rep_count):
+        tenant = jnp.where(request == i, request_tenant[i, 0], tenant)
+    slot = jnp.zeros_like(row)
+    for label in range(tenant_adapter_slot.shape[0]):
+        slot = jnp.where(tenant == label, tenant_adapter_slot[label], slot)
+    matched = slot == r
+
+    picked = lax.broadcasted_iota(jnp.int32, (rows, 2 * rows), 0)
+    place = lax.broadcasted_iota(jnp.int32, (rows, 2 * rows), 1)
+    source = (
+        lax.rem(picked // steps, tp_count) * (2 * steps * rows_rep)
+        + lax.rem(picked, steps) * rows_rep
+        + picked // group_rows
+    )
+
+    for copy in gathers:
+        copy.wait_recv()
+    everything = gathered[...].reshape(2 * rows, half_depth)
+    for h in range(2):
+        order = jnp.where(place == source + h * steps * rows_rep, 1.0, 0.0).astype(jnp.bfloat16)
+        hidden[:, h * half_depth : (h + 1) * half_depth] = jnp.dot(
+            order, everything, preferred_element_type=jnp.float32
+        ).astype(jnp.bfloat16)
+
+    load_down.wait()
+    low_send[...] = jnp.zeros_like(low_send)
+    low_send[:, 0:rank] = jnp.dot(hidden[...], down[...], preferred_element_type=jnp.float32)
+    low_copies = []
+    for d in range(tp_count):
+        to = lax.rem(t + d, tp_count)
+        source_rep = lax.rem(t + d, rep_count)
+        copy = remote(low_send, low_recv.at[r], low_send_sem.at[d], low_recv_sem.at[r], to, t)
+        arrival = remote(
+            low_send,
+            low_recv.at[source_rep],
+            low_send_sem.at[d],
+            low_recv_sem.at[source_rep],
+            to,
+            t,
+        )
+        low_copies.append((copy, arrival))
+        if d == 0:
+            pl.when(r != t)(copy.start)
+        else:
+            copy.start()
+
+    @pl.when(r == t)
+    def _():
+        low_recv[r] = low_send[...]
+
+    def multiply(c):
+        load_weights[c].wait()
+        return jnp.dot(hidden[...], weights[c], preferred_element_type=jnp.float32)
+
+    def send_parts(c, value):
+        part_send[c] = value.reshape(rep_count, group_rows, CHUNK)
+        for d in range(1, rep_count):
+            to = lax.rem(r + d, rep_count)
+            copy = remote(
+                part_send.at[c, to],
+                part_recv.at[c, r],
+                part_send_sem.at[c, to],
+                part_recv_sem.at[c, r],
+                t,
+                to,
+            )
+            copy.start()
+            sends.append(copy)
+
+    def total(c):
+        value = part_send[c, r]
+        for d in range(1, rep_count):
+            place = lax.rem(r + d, rep_count)
+            remote(
+                part_send.at[c, place],
+                part_recv.at[c, place],
+                part_send_sem.at[c, place],
+                part_recv_sem.at[c, place],
+                t,
+                place,
+            ).wait_recv()
+            value = value + part_recv[c, place]
+        return value
+
+    arrivals = {}
+
+    def send_rows(name, source_buffer, place_of, send_sem, recv_sem):
+        arrivals[name] = []
+        for d in range(tp_count - 1, 0, -1):
+            to = lax.rem(t + d, tp_count)
+            copy = remote(
+                source_buffer.at[to], place_of(t), send_sem.at[to], recv_sem.at[t], to, r
+            )
+            copy.start()
+            sends.append(copy)
+            arrivals[name].append(
+                remote(source_buffer.at[to], place_of(to), send_sem.at[to], recv_sem.at[to], to, r)
+            )
+
+    def finish_key_value():
+        value = total(0)
+        for place in range(tp_count):
+            for s in range(steps):
+                for h in range(chunk_heads):
+                    at = s * chunk_heads + h
+                    kv_send[place, at : at + 1, :] = value[
+                        place * steps + s : place * steps + s + 1,
+                        h * HEAD_SIZE : (h + 1) * HEAD_SIZE,
+                    ]
+        send_rows("kv", kv_send, lambda i: kv_recv.at[i], kv_send_sem, kv_recv_sem)
+        kv_recv[t] = kv_send[t]
+
+    per_group = query_columns // HEAD_SIZE // 2 // chunk_heads
+
+    def finish_query(c):
+        value = total(c + 1)
+        half, inside = c // per_group, c % per_group
+        for h in range(chunk_heads):
+            stage[half, :, inside * chunk_heads + h, :] = value[
+                :, h * HEAD_SIZE : (h + 1) * HEAD_SIZE
+            ]
+        if inside == per_group - 1:
+            query_send[half] = (
+                stage[half].astype(jnp.bfloat16).reshape(tp_count, steps, -1, HEAD_SIZE)
+            )
+            send_rows(
+                half,
+                query_send.at[half],
+                lambda i: query_recv.at[half, i],
+                query_send_sem.at[half],
+                query_recv_sem.at[half],
+            )
+            query_recv[half, t] = query_send[half, t]
+
+    def adapted(c, value):
+        return value + jnp.dot(
+            low_masked[...],
+            up[:, c * CHUNK : (c + 1) * CHUNK],
+            preferred_element_type=jnp.float32,
+        )
+
+    heads_of = per_group * chunk_heads
+
+    def attend_half(half):
+        if half == 0:
+            load_cache.wait()
+            for copy in arrivals["kv"]:
+                copy.wait_recv()
+        for copy in arrivals[half]:
+            copy.wait_recv()
+        length = cache_length[0]
+        scale = HEAD_SIZE**-0.5
+        valid = lax.broadcasted_iota(jnp.int32, (steps * heads_of, positions), 1) < length
+        extra = steps * chunk_heads
+        column = lax.broadcasted_iota(jnp.int32, (steps * heads_of, extra), 1)
+        step_of = lax.broadcasted_iota(jnp.int32, (steps * heads_of, extra), 0) // heads_of
+        causal = column // chunk_heads <= step_of
+        for tt in range(tp_count):
+            g = 2 * tt + half
+            query = query_recv[half, tt].reshape(steps * heads_of, HEAD_SIZE)
+            keys = cache[:, g * HEAD_SIZE : (g + 1) * HEAD_SIZE]
+            values = cache[:, half_width + g * HEAD_SIZE : half_width + (g + 1) * HEAD_SIZE]
+            holder, inner = g // chunk_heads, g % chunk_heads
+            new_keys = kv_recv[holder].astype(jnp.bfloat16)
+            new_values = kv_recv[tp_count // 2 + holder].astype(jnp.bfloat16).astype(jnp.float32)
+            contract = (((1,), (1,)), ((), ()))
+            older = (
+                lax.dot_general(query, keys, contract, preferred_element_type=jnp.float32) * scale
+            )
+            newer = (
+                lax.dot_general(query, new_keys, contract, preferred_element_type=jnp.float32)
+                * scale
+            )
+            older = jnp.where(valid, older, -jnp.inf)
+            newer = jnp.where(
+                causal & (lax.rem(column, chunk_heads) == inner), newer, -jnp.inf
+            )
+            top = jnp.maximum(
+                jnp.max(older, axis=1, keepdims=True), jnp.max(newer, axis=1, keepdims=True)
+            )
+            older = jnp.exp(older - top)
+            newer = jnp.exp(newer - top)
+            whole = jnp.sum(older, axis=1, keepdims=True) + jnp.sum(newer, axis=1, keepdims=True)
+            older = (older / whole).astype(jnp.bfloat16)
+            newer = (newer / whole).astype(jnp.bfloat16).astype(jnp.float32)
+            mixed = jnp.dot(older, values, preferred_element_type=jnp.float32)
+            for s in range(steps):
+                at = s * chunk_heads + inner
+                mixed = mixed + newer[:, at : at + 1] * new_values[at : at + 1, :]
+            mixed = mixed.astype(jnp.bfloat16)
+            for s in range(steps):
+                out[s, g * heads_of : (g + 1) * heads_of, :] = mixed[
+                    s * heads_of : (s + 1) * heads_of, :
+                ]
+
+    send_parts(0, multiply(0))
+    for c in range(DEFER):
+        held[c] = multiply(c + 1)
+    for d, (_, arrival) in enumerate(low_copies):
+        if d == 0:
+            pl.when(r != t)(arrival.wait_recv)
+        else:
+            arrival.wait_recv()
+    low_total = low_recv[0]
+    for i in range(1, rep_count):
+        low_total = low_total + low_recv[i]
+    low_masked[...] = jnp.where(matched, low_total, 0.0).astype(jnp.bfloat16)[:, 0:rank]
+    load_up.wait()
+    for c in range(DEFER):
+        send_parts(c + 1, adapted(c, held[c]))
+    finish_key_value()
+    for c in range(DEFER, query_chunks):
+        send_parts(c + 1, adapted(c, multiply(c + 1)))
+        finish_query(c - DEFER)
+    attended = per_group <= query_chunks - DEFER
+    if attended:
+        attend_half(0)
+    for c in range(query_chunks - DEFER, query_chunks):
+        finish_query(c)
+    if not attended:
+        attend_half(0)
+    attend_half(1)
+
+    for copy in sends:
+        copy.wait_send()
+    for d, (copy, _) in enumerate(low_copies):
+        if d == 0:
+            pl.when(r != t)(copy.wait_send)
+        else:
+            copy.wait_send()
+
+
+def fused(*operands):
+    tokens, query_weight, key_value_weight, down, up, request_tenant, slots, cache, lengths = operands
+    tp_count = lax.axis_size("tp")
+    rep_count = lax.axis_size("rep")
+    steps, rows_rep, depth = tokens.shape
+    columns = query_weight.shape[1]
+    chunks = columns // CHUNK + 1
+    group_rows = steps * tp_count
+    rows = group_rows * rep_count
+    heads_of = columns // HEAD_SIZE // 2
+    bf16, f32 = jnp.bfloat16, jnp.float32
+    dma = pltpu.SemaphoreType.DMA
+    anywhere = pl.BlockSpec(memory_space=pl.ANY)
+    scalars = pl.BlockSpec(memory_space=pltpu.SMEM)
+    heads = tp_count * columns // HEAD_SIZE
+    result = pl.pallas_call(
+        functools.partial(fused_kernel, tp_count, rep_count),
+        out_shape=jax.ShapeDtypeStruct((steps, heads, HEAD_SIZE), bf16),
+        in_specs=[anywhere] * 5 + [scalars] * 2 + [anywhere, scalars],
+        out_specs=pl.BlockSpec(memory_space=pltpu.VMEM),
+        scratch_shapes=[
+            pltpu.VMEM(tokens.shape, bf16),
+            pltpu.VMEM((2 * steps * rows_rep, depth // 2), f32),
+            pltpu.VMEM((tp_count, 2 * steps * rows_rep, depth // 2), bf16),
+            pltpu.VMEM((rows, depth), bf16),
+            pltpu.VMEM((chunks, depth, CHUNK), bf16),
+            pltpu.VMEM(down.shape[1:], bf16),
+            pltpu.VMEM(up.shape[1:], bf16),
+            pltpu.VMEM(cache.shape[1:], bf16),
+            pltpu.VMEM((rows, HEAD_SIZE), f32),
+            pltpu.VMEM((rep_count, rows, HEAD_SIZE), f32),
+            pltpu.VMEM((rows, down.shape[2]), bf16),
+            pltpu.VMEM((DEFER, rows, CHUNK), f32),
+            pltpu.VMEM((chunks, rep_count, group_rows, CHUNK), f32),
+            pltpu.VMEM((chunks, rep_count, group_rows, CHUNK), f32),
+            pltpu.VMEM((2, group_rows, heads_of, HEAD_SIZE), f32),
+            pltpu.VMEM((2, tp_count, steps, heads_of, HEAD_SIZE), bf16),
+            pltpu.VMEM((2, tp_count, steps, heads_of, HEAD_SIZE), bf16),
+            pltpu.VMEM((tp_count, steps * CHUNK // HEAD_SIZE, HEAD_SIZE), f32),
+            pltpu.VMEM((tp_count, steps * CHUNK // HEAD_SIZE, HEAD_SIZE), f32),
+            dma((chunks,)),
+            dma((4,)),
+            dma((tp_count,)),
+            dma((tp_count,)),
+            dma((tp_count,)),
+            dma((rep_count,)),
+            dma((chunks, rep_count)),
+            dma((chunks, rep_count)),
+            dma((2, tp_count)),
+            dma((2, tp_count)),
+            dma((tp_count,)),
+            dma((tp_count,)),
+        ],
+        compiler_params=pltpu.CompilerParams(
+            collective_id=0, has_side_effects=True, vmem_limit_bytes=60 * 1024 * 1024
+        ),
+    )(*operands)
+    return result.reshape(steps, 1, heads * HEAD_SIZE)
+
+
+def fits(tokens, query_weight, key_value_weight, down, up, request_tenant, slots, cache, lengths):
+    tp_count = lax.axis_size("tp")
+    rep_count = lax.axis_size("rep")
+    columns = query_weight.shape[1]
+    return (
+        tp_count == rep_count
+        and tp_count % 2 == 0
+        and tokens.shape[0] == 2
+        and tokens.shape[0] * tp_count == 8
+        and tokens.shape[1] == rep_count
+        and down.shape[0] == 1
+        and up.shape[0] == 1
+        and cache.shape[0] == 1
+        and key_value_weight.shape[1] == CHUNK
+        and columns == 2 * 16 * HEAD_SIZE
+        and tokens.shape[2] <= 4096
+    )
 
 
 def slot_lookup(request_tenant, tenant_adapter_slot):
@@ -71,6 +520,19 @@
     key_value_cache,
     cache_length_per_row,
 ):
+    operands = (
+        tokens,
+        query_weight,
+        key_value_weight,
+        adapter_down_weight,
+        adapter_up_weight,
+        request_tenant,
+        tenant_adapter_slot,
+        key_value_cache,
+        cache_length_per_row,
+    )
+    if fits(*operands):
+        return fused(*operands)
     tp_count = lax.axis_size("tp")
     rep_count = lax.axis_size("rep")
     rep_place = lax.axis_index("rep")

time: 101 us -> 47 us (0.47)
  blocking collectives: 56 us -> 0 us
  Pallas kernels: 0 us -> 41.1 us
  matrix products: 19.7 us -> 0 us
  waiting for transfers between devices: 9.03 us -> 0 us
  starting transfers between devices: 8.37 us -> 0 us
  other arithmetic: 1.35 us -> 0 us
    pallas_call x0 -> x1, Pallas kernels: none -> 41.1 us  [fused(): pl.pallas_call(functools.partial(fused_kernel, tp_count, rep_count), out_...]
    all_gather x2 -> x0, blocking collectives: 28.8 us -> none  [the longest x1 15.6 us: shards(): piece = lax.all_gather(tokens, 'tp', axis=1, tiled=True)]
    dot_general x11 -> x0, matrix products: 19.7 us -> none  [the longest x1 13.5 us: shards(): jnp.dot(flat, query_weight, preferred_element_type=jnp.float32)]
    unnamed x1 -> x0, blocking collectives: 17.1 us -> none
    psum x1 -> x0, blocking collectives: 10.1 us -> none  [shards(): low_sum = lax.psum(low_part, 'rep')]
    all_to_all x2 -> x0, waiting for transfers between devices: 9.03 us -> none  [the longest x1 5.7 us: shards(): lax.all_to_all(q_sum.astype(jnp.bfloat16), 'tp', split_axis=1, concat_axi...]
    all_to_all x2 -> x0, starting transfers between devices: 8.37 us -> none  [the longest x1 5.09 us: shards(): lax.all_to_all(kv_sum.astype(jnp.bfloat16), 'tp', split_axis=1, concat_ax...]
    convert_element_type x5 -> x0, local copies, waits for them, and re-layouts: 2.72 us -> none  [the longest x2 1.37 us: shards(): q_sum.astype(jnp.bfloat16)]
  transfers between devices with their start and end apart: 2 -> 0, of which waited for: 2 -> 0; matrix products, arithmetic and copies ran while one was open for 2% -> 0% of each run, Pallas kernels for 0% -> 0%
where the time goes in v1:
time: 47 us; the launch traced here: 46.8 us
  Pallas kernels  41.1 us (87%)
  local copies, waits for them, and re-layouts  5.06 us (11%)
  between operations  0.66 us (1%)
    pallas_call x1, Pallas kernels, fused(): pl.pallas_call(functools.partial(fused_kernel, tp_count, rep_count), out_...  41.1 us
    unnamed x2, local copies, waits for them, and re-layouts  3.57 us
    reshape x1, local copies, waits for them, and re-layouts, fused(): return result.reshape(steps, 1, heads * HEAD_SIZE)  1.49 us

profile of v1, /device:TPU:0, one launch (start us, length us, event | category | flops | bytes accessed | tf_op | source)
XLA Modules:
  0.0 46.8 jit_solution(8096511539417487639)
XLA Ops:
  0.7 1.3 %copy.11.request_tenant = s32[16,1]{1,0:T(8,128)} copy(s32[16,1]{0,1:T(1,128)} %param.14) | data formatting | bytes 128 | tf_op args[5]
  2.0 2.2 %copy.10.adapter_down_weight = bf16[1,4096,16]{2,1,0:T(8,128)(2,1)} copy(bf16[1,4096,16]{1,2,0:T(8,128)(2,1)} %param.12) | data formatting | bytes 262144 | tf_op args[3]
  4.2 41.1 %shard_map.91 = bf16[2,128,128]{2,1,0:T(8,128)(2,1)} custom-call(bf16[2,4,4096]{2,1,0:T(4,128)(2,1)} %tokens.1, bf16[4096,4096]{1,0:T(8,128)(2,1)} %query_weight.1, bf16[4096,512]{1,0:T(8,128)(2,1)} %key_value_weight.1, bf16[1,4096,16]{2,1,0:T(8,128)(2,1)} %copy.10.adapter_down_weight, bf16[1,16,4096]{2,1,0:T(8,128)(2,1)} %adapter_up_weight.1, ...), custom_call_target="tpu_custom_call" | custom-call | tf_op jit(solution)/shard_map/pallas_call | solution.py:395
  45.3 1.5 %reshape.3 = bf16[2,1,16384]{2,0,1:T(2,128)(2,1)} reshape(bf16[2,128,128]{2,1,0:T(8,128)(2,1)} %shard_map.91) | data formatting | bytes 131072 | tf_op jit(solution)/shard_map/reshape | solution.py:437

commit v2 on v1

--- a/solution.py
+++ b/solution.py
@@ -11,6 +11,8 @@
 HEAD_SIZE = 128
 CHUNK = 512
 DEFER = 2
+BEFORE = 2
+AHEAD = 3
 MESH = pl.DeviceIdType.MESH
 
 
@@ -61,6 +63,7 @@
     query_recv,
     kv_send,
     kv_recv,
+    mix,
     weight_sem,
     load_sem,
     gather_send_sem,
@@ -83,7 +86,7 @@
     query_columns = query_weight.shape[1]
     query_chunks = query_columns // CHUNK
     chunk_heads = CHUNK // HEAD_SIZE
-    rank = adapter_down_weight.shape[2]
+    rank = adapter_down_weight.shape[1]
     positions = key_value_cache.shape[1]
     half_width = KEY_VALUE_HEADS * HEAD_SIZE
 
@@ -112,11 +115,17 @@
         )
         for c in range(query_chunks)
     ]
-    load_weights[0].start()
     load_up.start()
-    for copy in load_weights[1:]:
-        copy.start()
-    load_cache.start()
+    started = []
+
+    def start_until(count):
+        while len(started) < min(count, query_chunks + 1):
+            load_weights[len(started)].start()
+            started.append(True)
+            if len(started) == query_chunks + 1:
+                load_cache.start()
+
+    start_until(BEFORE)
 
     load_tokens.wait()
     for s in range(steps):
@@ -142,11 +151,13 @@
             )
         )
 
+    start_until(AHEAD)
+
     row = lax.broadcasted_iota(jnp.int32, (rows, HEAD_SIZE), 0)
     request = lax.rem(row // steps, tp_count) * rep_count + row // group_rows
     tenant = jnp.zeros_like(row)
     for i in range(tp_count * rep_count):
-        tenant = jnp.where(request == i, request_tenant[i, 0], tenant)
+        tenant = jnp.where(request == i, request_tenant[0, i], tenant)
     slot = jnp.zeros_like(row)
     for label in range(tenant_adapter_slot.shape[0]):
         slot = jnp.where(tenant == label, tenant_adapter_slot[label], slot)
@@ -171,7 +182,9 @@
 
     load_down.wait()
     low_send[...] = jnp.zeros_like(low_send)
-    low_send[:, 0:rank] = jnp.dot(hidden[...], down[...], preferred_element_type=jnp.float32)
+    low_send[:, 0:rank] = lax.dot_general(
+        hidden[...], down[...], (((1,), (1,)), ((), ())), preferred_element_type=jnp.float32
+    )
     low_copies = []
     for d in range(tp_count):
         to = lax.rem(t + d, tp_count)
@@ -197,6 +210,7 @@
 
     def multiply(c):
         load_weights[c].wait()
+        start_until(c + 1 + AHEAD)
         return jnp.dot(hidden[...], weights[c], preferred_element_type=jnp.float32)
 
     def send_parts(c, value):
@@ -334,11 +348,12 @@
             for s in range(steps):
                 at = s * chunk_heads + inner
                 mixed = mixed + newer[:, at : at + 1] * new_values[at : at + 1, :]
-            mixed = mixed.astype(jnp.bfloat16)
-            for s in range(steps):
-                out[s, g * heads_of : (g + 1) * heads_of, :] = mixed[
-                    s * heads_of : (s + 1) * heads_of, :
-                ]
+            mix[g] = mixed
+            for m in range(heads_of):
+                at = (g * heads_of + m) * HEAD_SIZE
+                out[:, at : at + HEAD_SIZE] = mix[g, pl.ds(m, steps, stride=heads_of), :].astype(
+                    jnp.bfloat16
+                )
 
     send_parts(0, multiply(0))
     for c in range(DEFER):
@@ -387,6 +402,7 @@
     group_rows = steps * tp_count
     rows = group_rows * rep_count
     heads_of = columns // HEAD_SIZE // 2
+    rank = down.shape[2]
     bf16, f32 = jnp.bfloat16, jnp.float32
     dma = pltpu.SemaphoreType.DMA
     anywhere = pl.BlockSpec(memory_space=pl.ANY)
@@ -394,7 +410,7 @@
     heads = tp_count * columns // HEAD_SIZE
     result = pl.pallas_call(
         functools.partial(fused_kernel, tp_count, rep_count),
-        out_shape=jax.ShapeDtypeStruct((steps, heads, HEAD_SIZE), bf16),
+        out_shape=jax.ShapeDtypeStruct((steps, heads * HEAD_SIZE), bf16),
         in_specs=[anywhere] * 5 + [scalars] * 2 + [anywhere, scalars],
         out_specs=pl.BlockSpec(memory_space=pltpu.VMEM),
         scratch_shapes=[
@@ -403,12 +419,12 @@
             pltpu.VMEM((tp_count, 2 * steps * rows_rep, depth // 2), bf16),
             pltpu.VMEM((rows, depth), bf16),
             pltpu.VMEM((chunks, depth, CHUNK), bf16),
-            pltpu.VMEM(down.shape[1:], bf16),
+            pltpu.VMEM((rank, depth), bf16),
             pltpu.VMEM(up.shape[1:], bf16),
             pltpu.VMEM(cache.shape[1:], bf16),
             pltpu.VMEM((rows, HEAD_SIZE), f32),
             pltpu.VMEM((rep_count, rows, HEAD_SIZE), f32),
-            pltpu.VMEM((rows, down.shape[2]), bf16),
+            pltpu.VMEM((rows, rank), bf16),
             pltpu.VMEM((DEFER, rows, CHUNK), f32),
             pltpu.VMEM((chunks, rep_count, group_rows, CHUNK), f32),
             pltpu.VMEM((chunks, rep_count, group_rows, CHUNK), f32),
@@ -417,6 +433,7 @@
             pltpu.VMEM((2, tp_count, steps, heads_of, HEAD_SIZE), bf16),
             pltpu.VMEM((tp_count, steps * CHUNK // HEAD_SIZE, HEAD_SIZE), f32),
             pltpu.VMEM((tp_count, steps * CHUNK // HEAD_SIZE, HEAD_SIZE), f32),
+            pltpu.VMEM((2 * tp_count, steps * heads_of, HEAD_SIZE), f32),
             dma((chunks,)),
             dma((4,)),
             dma((tp_count,)),
@@ -433,7 +450,17 @@
         compiler_params=pltpu.CompilerParams(
             collective_id=0, has_side_effects=True, vmem_limit_bytes=60 * 1024 * 1024
         ),
-    )(*operands)
+    )(
+        tokens,
+        query_weight,
+        key_value_weight,
+        jnp.transpose(down, (0, 2, 1)),
+        up,
+        jnp.transpose(request_tenant),
+        slots,
+        cache,
+        lengths,
+    )
     return result.reshape(steps, 1, heads * HEAD_SIZE)
 
 

time: 47 us -> 39.7 us (0.84)
  Pallas kernels: 41.1 us -> 37.3 us
  local copies, waits for them, and re-layouts: 5.06 us -> 1.52 us
    pallas_call x1, Pallas kernels: 41.1 us -> 37.3 us  [fused(): pl.pallas_call(functools.partial(fused_kernel, tp_count, rep_count), out_...]
    unnamed x2 -> x1, local copies, waits for them, and re-layouts: 3.57 us -> 1.52 us
    reshape x1 -> x0, local copies, waits for them, and re-layouts: 1.49 us -> none  [fused(): return result.reshape(steps, 1, heads * HEAD_SIZE)]
where the time goes in v2:
time: 39.7 us; the launch traced here: 39.5 us
  Pallas kernels  37.3 us (94%)
  local copies, waits for them, and re-layouts  1.52 us (4%)
  between operations  0.66 us (2%)
    pallas_call x1, Pallas kernels, fused(): pl.pallas_call(functools.partial(fused_kernel, tp_count, rep_count), out_...  37.3 us
    unnamed x1, local copies, waits for them, and re-layouts  1.52 us

profile of v2, /device:TPU:0, one launch (start us, length us, event | category | flops | bytes accessed | tf_op | source)
XLA Modules:
  0.0 39.5 jit_solution(3125226647772293609)
XLA Ops:
  0.7 37.3 %shard_map.91 = bf16[2,16384]{1,0:T(2,128)(2,1)} custom-call(bf16[2,4,4096]{2,1,0:T(4,128)(2,1)} %tokens.1, bf16[4096,4096]{1,0:T(8,128)(2,1)} %query_weight.1, bf16[4096,512]{1,0:T(8,128)(2,1)} %key_value_weight.1, bf16[1,16,4096]{2,1,0:T(8,128)(2,1)} %bitcast.4, bf16[1,16,4096]{2,1,0:T(8,128)(2,1)} %adapter_up_weight.1, s32[1,16]{1,0:T(1,128)} %bitcast.5, ...), custom_call_target="tpu_custom_call" | custom-call | tf_op jit(solution)/shard_map/pallas_call | solution.py:411
  38.0 1.5 %copy.12 = bf16[2,1,16384]{2,0,1:T(2,128)(2,1)} copy(bf16[2,1,16384]{2,0,1:T(2,128)(2,1)} %bitcast.3) | data formatting | bytes 131072

commit v3 on v2

--- a/solution.py
+++ b/solution.py
@@ -11,8 +11,9 @@
 HEAD_SIZE = 128
 CHUNK = 512
 DEFER = 2
+LAG = 8
 BEFORE = 2
-AHEAD = 3
+AHEAD = 9
 MESH = pl.DeviceIdType.MESH
 
 
@@ -370,17 +371,21 @@
     load_up.wait()
     for c in range(DEFER):
         send_parts(c + 1, adapted(c, held[c]))
-    finish_key_value()
+    finished = 0
     for c in range(DEFER, query_chunks):
         send_parts(c + 1, adapted(c, multiply(c + 1)))
-        finish_query(c - DEFER)
-    attended = per_group <= query_chunks - DEFER
-    if attended:
-        attend_half(0)
-    for c in range(query_chunks - DEFER, query_chunks):
-        finish_query(c)
-    if not attended:
-        attend_half(0)
+        if c >= LAG:
+            if c == LAG:
+                finish_key_value()
+            finish_query(finished)
+            finished += 1
+    if finished == 0:
+        finish_key_value()
+    while finished < query_chunks - 1:
+        finish_query(finished)
+        finished += 1
+    attend_half(0)
+    finish_query(finished)
     attend_half(1)
 
     for copy in sends:

time: 39.7 us -> 39.3 us (0.990)
  no operation moved by 1% of the time
where the time goes in v3:
time: 39.3 us; the launch traced here: 39.1 us
  Pallas kernels  37 us (94%)
  local copies, waits for them, and re-layouts  1.52 us (4%)
  between operations  0.66 us (2%)
    pallas_call x1, Pallas kernels, fused(): pl.pallas_call(functools.partial(fused_kernel, tp_count, rep_count), out_...  37 us
    unnamed x1, local copies, waits for them, and re-layouts  1.52 us

profile of v3, /device:TPU:0, one launch (start us, length us, event | category | flops | bytes accessed | tf_op | source)
XLA Modules:
  0.0 39.1 jit_solution(2161471184997367104)
XLA Ops:
  0.7 37.0 %shard_map.91 = bf16[2,16384]{1,0:T(2,128)(2,1)} custom-call(bf16[2,4,4096]{2,1,0:T(4,128)(2,1)} %tokens.1, bf16[4096,4096]{1,0:T(8,128)(2,1)} %query_weight.1, bf16[4096,512]{1,0:T(8,128)(2,1)} %key_value_weight.1, bf16[1,16,4096]{2,1,0:T(8,128)(2,1)} %bitcast.4, bf16[1,16,4096]{2,1,0:T(8,128)(2,1)} %adapter_up_weight.1, s32[1,16]{1,0:T(1,128)} %bitcast.5, ...), custom_call_target="tpu_custom_call" | custom-call | tf_op jit(solution)/shard_map/pallas_call | solution.py:416
  37.6 1.5 %copy.12 = bf16[2,1,16384]{2,0,1:T(2,128)(2,1)} copy(bf16[2,1,16384]{2,0,1:T(2,128)(2,1)} %bitcast.3) | data formatting | bytes 131072
